TPU v7x, 32 devices: a whole 2x2x4 slice. The times are simulated.
32 devices in a mesh: groups: 2 (over y), row: 4 (over z), col: 4 (over x, core).
Axes of the slice: x: 2, y: 2, z: 4, core: 2. Of those that a mesh axis runs over, the one named last changes fastest.
Arguments:
- a_blocks: bfloat16 [8, 4, 16, 128, 128], P(('groups', 'row'), 'col'), parts along dimension 0, may hold values from -0.5 to 0.5
- a_index: int32 [8, 4, 2, 16], P(('groups', 'row'), 'col'), parts along dimension 0, may hold values from 0 to 7, as said below
- a_live: int32 [8, 4], P(('groups', 'row'), 'col'), parts along dimension 0, may hold values from 4 to 16, as said below
- b_blocks: bfloat16 [8, 4, 1, 3, 128, 128], P(('groups', 'row'), 'col'), parts along dimension 0, may hold values from -6 to 6
- b_index: int32 [8, 4, 1, 2, 3], P(('groups', 'row'), 'col'), parts along dimension 0, may hold values from 0 to 7, as said below
- c_keep: int32 [32, 8], P(('groups', 'col'), 'row'), parts along dimension 0, may hold values 0 or 1
Outputs:
- c_out: bfloat16 [4096, 1024], P(('groups', 'col'), 'row'), parts along dimension 0
There are 2 independent parts, one for each index of `groups`. A program takes and returns all parts, laid end to end along the dimension named above; each array names one. Nothing has to cross between parts.
Inputs may be any that keep to these rules, and one draw needn't show every extreme that they name: `a_index`: within one panel the pairs (block row, inner block) are distinct; block rows are below 4, inner blocks below 8. `a_live`: some panel holds all 16 slots in every draw. `b_index`: within one panel the pairs (inner block, block column) are distinct; inner blocks are below 8, block columns below 2.
All inputs are finite; a program needn't handle non-finite values. No bound on the sum of `c_keep` on one device may be relied on, other than what follows from the above.
Results may differ from a plain program's by a relative error of at most 0.001.
Values may be sent and summed in bfloat16 or wider, within the bound.
A program may use at most 64 MiB of HBM per device.

v0:
```python
import jax
import jax.numpy as jnp
from jax import lax
from jax.sharding import PartitionSpec as P

BS = 128
MR = 4
NC = 2
KP = 8
NZA = 16
NZB = 3


def as_sent(array):
    return jax.tree.map(lambda a: a.astype(jnp.bfloat16) if a.dtype == jnp.float32 else a, array)


def passed_along(value, axis, steps):
    count = lax.axis_size(axis)
    pairs = [(source, (source + steps) % count) for source in range(count)]
    return lax.ppermute(value, axis, pairs)


def panel_product(total, first_blocks, first_index, first_live, second_blocks, second_index):
    slot_ids = second_index[0] * NC + second_index[1]
    slot_range = jnp.arange(KP * NC, dtype=jnp.int32)
    picker = (slot_range[:, None] == slot_ids[None, :]).astype(jnp.bfloat16).reshape(KP, NC, NZB)
    dense_b = jnp.einsum(
        "kcz,zuv->kucv", picker, second_blocks, preferred_element_type=jnp.bfloat16
    )
    dense_b = dense_b.reshape(KP * BS, NC * BS)
    live_mask = (jnp.arange(NZA, dtype=jnp.int32) < first_live).astype(jnp.bfloat16)
    row_hot = (jnp.arange(MR, dtype=jnp.int32)[:, None] == first_index[0][None, :]).astype(
        jnp.bfloat16
    )
    inner_hot = (jnp.arange(KP, dtype=jnp.int32)[:, None] == first_index[1][None, :]).astype(
        jnp.bfloat16
    )
    placer = row_hot[:, None, :] * inner_hot[None, :, :] * live_mask[None, None, :]
    dense_a = jnp.einsum("rkz,zuv->rukv", placer, first_blocks, preferred_element_type=jnp.bfloat16)
    dense_a = dense_a.reshape(MR * BS, KP * BS)
    return total + jnp.dot(dense_a, dense_b, preferred_element_type=jnp.float32)


def local(a_blocks, a_index, a_live, b_blocks, b_index, c_keep):
    row_count = lax.axis_size("row")
    col_count = lax.axis_size("col")
    row_pos = lax.axis_index("row")
    col_pos = lax.axis_index("col")
    tick_total = min(6, row_count)
    bit_total = col_count.bit_length() - 1
    a_state = (a_blocks, a_index, a_live)
    for bit_pos in range(bit_total):
        shifted = jax.tree.map(
            lambda part, own: part.astype(own.dtype),
            passed_along(as_sent(a_state), "row", -(1 << bit_pos)),
            a_state,
        )
        take_bit = col_pos // (1 << bit_pos) % 2 == 1
        a_state = jax.tree.map(
            lambda incoming, current: jnp.where(take_bit, incoming, current), shifted, a_state
        )
    skew_amount = row_pos % col_count
    b_state = (b_blocks, b_index)
    for bit_pos in range(bit_total):
        shifted = jax.tree.map(
            lambda part, own: part.astype(own.dtype),
            passed_along(as_sent(b_state), "col", -(1 << bit_pos)),
            b_state,
        )
        take_bit = skew_amount // (1 << bit_pos) % 2 == 1
        b_state = jax.tree.map(
            lambda incoming, current: jnp.where(take_bit, incoming, current), shifted, b_state
        )
    total = jnp.zeros((MR * BS, NC * BS), jnp.float32)
    for tick_no in range(tick_total):
        panel_id = (col_pos + row_pos + tick_no) % row_count
        depth_id = panel_id // col_count
        group_blocks = b_state[0][0, 0]
        group_index = b_state[1][0, 0]
        second_blocks = lax.dynamic_index_in_dim(group_blocks, depth_id, 0, keepdims=False)
        second_index = lax.dynamic_index_in_dim(group_index, depth_id, 0, keepdims=False)
        first_blocks, first_index, first_live = a_state
        total = panel_product(
            total,
            first_blocks[0, 0],
            first_index[0, 0],
            first_live[0, 0],
            second_blocks,
            second_index,
        )
        if tick_no + 1 < tick_total:
            a_state = jax.tree.map(
                lambda part, own: part.astype(own.dtype),
                passed_along(as_sent(a_state), "row", -1),
                a_state,
            )
            b_state = jax.tree.map(
                lambda part, own: part.astype(own.dtype),
                passed_along(as_sent(b_state), "col", -1),
                b_state,
            )
    keep_mask = c_keep.astype(jnp.float32)
    filtered = total.reshape(MR, BS, NC, BS) * keep_mask[:, None, :, None]
    return filtered.reshape(MR * BS, NC * BS).astype(jnp.bfloat16)


def solution(mesh):
    placed = (
        P(("groups", "row"), "col", None, None, None),
        P(("groups", "row"), "col", None, None),
        P(("groups", "row"), "col"),
        P(("groups", "row"), "col", None, None, None, None),
        P(("groups", "row"), "col", None, None, None),
        P(("groups", "col"), "row"),
    )
    return jax.shard_map(
        local, mesh=mesh, in_specs=placed, out_specs=P(("groups", "col"), "row"), check_vma=False
    )
```

profile of v0, /device:TPU:0, one launch (start us, length us, event | category | flops | bytes accessed | tf_op | source)
XLA Modules:
  0.0 152.1 jit_solution(7808340706904303026)
XLA Ops:
  0.0 1.4 copy.12
  1.4 5.1 %collective-permute-start = (bf16[1,1,16,128,128]{4,2,3,1,0:T(8,128)(2,1)S(1)}, bf16[1,1,16,128,128]{4,2,3,1,0:T(8,128)(2,1)S(1)}, u32[]{:S(2)}, u32[]{:S(2)}) collective-permute-start(bf16[1,1,16,128,128]{4,2,3,1,0:T(8,128)(2,1)S(1)} %copy.12), channel_id=1, source_target_pairs={{0,12},{4,0},{8,4},{12,8},{1,13},{5,1},{9,5},{13,9},{2,14},{6,2},{... | collective-permute-start | bytes 1572872 | tf_op jit(solution)/shard_map/ppermute | solution.py:21
  6.5 0.4 collective-permute-start.4
  7.0 0.4 collective-permute-start.2
  7.7 1.5 collective-permute-start.8
  10.0 0.7 copy-done.4
  10.7 7.1 %collective-permute-done.4 = s32[1,1]{1,0:T(1,128)} collective-permute-done((s32[1,1]{1,0:T(1,128)}, s32[1,1]{1,0:T(1,128)}, u32[]{:S(2)}, u32[]{:S(2)}) %collective-permute-start.4) | collective-permute-done | bytes 36 | tf_op jit(solution)/shard_map/ppermute | solution.py:21
  18.4 2.8 %collective-permute-start.5 = (s32[1,1]{1,0:T(1,128)}, s32[1,1]{1,0:T(1,128)}, u32[]{:S(2)}, u32[]{:S(2)}) collective-permute-start(s32[1,1]{1,0:T(1,128)} %select_n.137), channel_id=1, source_target_pairs={{0,8},{4,12},{8,0},{12,4},{1,9},{5,13},{9,1},{13,5},{2,10},{6,14},... | collective-permute-start | bytes 20 | tf_op jit(solution)/shard_map/ppermute | solution.py:21
  21.2 1.7 %collective-permute-done.5 = s32[1,1]{1,0:T(1,128)} collective-permute-done((s32[1,1]{1,0:T(1,128)}, s32[1,1]{1,0:T(1,128)}, u32[]{:S(2)}, u32[]{:S(2)}) %collective-permute-start.5) | collective-permute-done | bytes 36 | tf_op jit(solution)/shard_map/ppermute | solution.py:21
  23.5 5.6 %collective-permute-start.12 = (s32[1,1]{1,0:T(1,128)}, s32[1,1]{1,0:T(1,128)}, u32[]{:S(2)}, u32[]{:S(2)}) collective-permute-start(s32[1,1]{1,0:T(1,128)} %select_n.138), channel_id=1, source_target_pairs={{0,12},{4,0},{8,4},{12,8},{1,13},{5,1},{9,5},{13,9},{2,14},{6,2},{... | collective-permute-start | bytes 20 | tf_op jit(solution)/shard_map/ppermute | solution.py:21
  29.1 0.6 compare_convert_fusion.2
  29.8 4.0 %collective-permute-start.17 = (s32[1,1]{1,0:T(1,128)}, s32[1,1]{1,0:T(1,128)}, u32[]{:S(2)}, u32[]{:S(2)}) collective-permute-start(s32[1,1]{1,0:T(1,128)} %collective-permute-done.12), channel_id=1, source_target_pairs={{0,12},{4,0},{8,4},{12,8},{1,13},{5,1},{9,5},{13,9},{2,14},{6,2},{... | collective-permute-start | bytes 20 | tf_op jit(solution)/shard_map/ppermute | solution.py:21
  33.8 1.4 collective-permute-done.17
  35.2 0.6 compare_convert_fusion.1
  35.8 4.0 %collective-permute-start.22 = (s32[1,1]{1,0:T(1,128)}, s32[1,1]{1,0:T(1,128)}, u32[]{:S(2)}, u32[]{:S(2)}) collective-permute-start(s32[1,1]{1,0:T(1,128)} %collective-permute-done.17), channel_id=1, source_target_pairs={{0,12},{4,0},{8,4},{12,8},{1,13},{5,1},{9,5},{13,9},{2,14},{6,2},{... | collective-permute-start | bytes 20 | tf_op jit(solution)/shard_map/ppermute | solution.py:21
  39.8 1.4 collective-permute-done.22
  41.2 0.6 compare_convert_fusion
  41.9 1.6 %collective-permute-start.9 = (s32[1,1,1,2,3]{4,3,2,1,0:T(2,128)S(1)}, s32[1,1,1,2,3]{4,3,2,1,0:T(2,128)S(1)}, u32[]{:S(2)}, u32[]{:S(2)}) collective-permute-start(s32[1,1,1,2,3]{4,3,2,1,0:T(2,128)S(1)} %broadcast_select_fusion.4), channel_id=1, source_target_pairs={{0,2},{1,3},{2,0},{3,1},{4,6},{5,7},{6,4},{7,5},{8,10},{9,11},{10,... | collective-permute-start | bytes 80 | tf_op jit(solution)/shard_map/ppermute | solution.py:21
  43.4 2.1 %collective-permute-done.9 = s32[1,1,1,2,3]{4,3,2,1,0:T(2,128)S(1)} collective-permute-done((s32[1,1,1,2,3]{4,3,2,1,0:T(2,128)S(1)}, s32[1,1,1,2,3]{4,3,2,1,0:T(2,128)S(1)}, u32[]{:S(2)}, u32[]{:S(2)}) %collective-permute-start.9) | collective-permute-done | bytes 56 | tf_op jit(solution)/shard_map/ppermute | solution.py:21
  45.6 1.3 collective-permute-done.14
  46.9 1.7 %collective-permute-start.19 = (s32[1,1,1,2,3]{4,3,2,1,0:T(2,128)S(1)}, s32[1,1,1,2,3]{4,3,2,1,0:T(2,128)S(1)}, u32[]{:S(2)}, u32[]{:S(2)}) collective-permute-start(s32[1,1,1,2,3]{4,3,2,1,0:T(2,128)S(1)} %collective-permute-done.14), channel_id=1, source_target_pairs={{0,3},{1,0},{2,1},{3,2},{4,7},{5,4},{6,5},{7,6},{8,11},{9,8},{10,9... | collective-permute-start | bytes 80 | tf_op jit(solution)/shard_map/ppermute | solution.py:21
  48.6 1.3 collective-permute-done.19
  49.9 1.7 %collective-permute-start.24 = (s32[1,1,1,2,3]{4,3,2,1,0:T(2,128)S(1)}, s32[1,1,1,2,3]{4,3,2,1,0:T(2,128)S(1)}, u32[]{:S(2)}, u32[]{:S(2)}) collective-permute-start(s32[1,1,1,2,3]{4,3,2,1,0:T(2,128)S(1)} %collective-permute-done.19), channel_id=1, source_target_pairs={{0,3},{1,0},{2,1},{3,2},{4,7},{5,4},{6,5},{7,6},{8,11},{9,8},{10,9... | collective-permute-start | bytes 80 | tf_op jit(solution)/shard_map/ppermute | solution.py:21
  51.6 0.7 collective-permute-start.3
  52.3 0.5 collective-permute-done.24
  52.9 3.2 %collective-permute-done.3 = s32[1,1,2,16]{3,2,1,0:T(2,128)S(1)} collective-permute-done((s32[1,1,2,16]{3,2,1,0:T(2,128)S(1)}, s32[1,1,2,16]{3,2,1,0:T(2,128)S(1)}, u32[]{:S(2)}, u32[]{:S(2)}) %collective-permute-start.3) | collective-permute-done | bytes 160 | tf_op jit(solution)/shard_map/ppermute | solution.py:21
  56.0 4.0 %collective-permute-start.11 = (s32[1,1,2,16]{3,2,1,0:T(2,128)S(1)}, s32[1,1,2,16]{3,2,1,0:T(2,128)S(1)}, u32[]{:S(2)}, u32[]{:S(2)}) collective-permute-start(s32[1,1,2,16]{3,2,1,0:T(2,128)S(1)} %broadcast_select_fusion.7), channel_id=1, source_target_pairs={{0,12},{4,0},{8,4},{12,8},{1,13},{5,1},{9,5},{13,9},{2,14},{6,2},{... | collective-permute-start | bytes 392 | tf_op jit(solution)/shard_map/ppermute | solution.py:21
  60.1 1.3 collective-permute-done.11
  61.4 4.1 %collective-permute-start.16 = (s32[1,1,2,16]{3,2,1,0:T(2,128)S(1)}, s32[1,1,2,16]{3,2,1,0:T(2,128)S(1)}, u32[]{:S(2)}, u32[]{:S(2)}) collective-permute-start(s32[1,1,2,16]{3,2,1,0:T(2,128)S(1)} %collective-permute-done.11), channel_id=1, source_target_pairs={{0,12},{4,0},{8,4},{12,8},{1,13},{5,1},{9,5},{13,9},{2,14},{6,2},{... | collective-permute-start | bytes 392 | tf_op jit(solution)/shard_map/ppermute | solution.py:21
  65.5 1.3 collective-permute-done.16
  66.8 4.1 %collective-permute-start.21 = (s32[1,1,2,16]{3,2,1,0:T(2,128)S(1)}, s32[1,1,2,16]{3,2,1,0:T(2,128)S(1)}, u32[]{:S(2)}, u32[]{:S(2)}) collective-permute-start(s32[1,1,2,16]{3,2,1,0:T(2,128)S(1)} %collective-permute-done.16), channel_id=1, source_target_pairs={{0,12},{4,0},{8,4},{12,8},{1,13},{5,1},{9,5},{13,9},{2,14},{6,2},{... | collective-permute-start | bytes 392 | tf_op jit(solution)/shard_map/ppermute | solution.py:21
  71.0 1.3 collective-permute-done.21
  72.4 1.6 %collective-permute-start.7 = (bf16[1,1,1,3,128,128]{5,3,4,2,1,0:T(4,128)(2,1)S(1)}, bf16[1,1,1,3,128,128]{5,3,4,2,1,0:T(4,128)(2,1)S(1)}, u32[]{:S(2)}, u32[]{:S(2)}) collective-permute-start(bf16[1,1,1,3,128,128]{5,3,4,2,1,0:T(4,128)(2,1)S(1)} %broadcast_select_fusion.2), channel_id=1, source_target_pairs={{0,2},{1,3},{2,0},{3,1},{4,6},{5,7},{6,4},{7,5},{8,10},{9,11},{10,... | collective-permute-start | bytes 294920 | tf_op jit(solution)/shard_map/ppermute | solution.py:21
  74.0 3.5 %collective-permute-done.7 = bf16[1,1,1,3,128,128]{5,3,4,2,1,0:T(4,128)(2,1)S(1)} collective-permute-done((bf16[1,1,1,3,128,128]{5,3,4,2,1,0:T(4,128)(2,1)S(1)}, bf16[1,1,1,3,128,128]{5,3,4,2,1,0:T(4,128)(2,1)S(1)}, u32[]{:S(2)}, u32[]{:S(2)}) %collective-permute-start.7) | collective-permute-done | bytes 98336 | tf_op jit(solution)/shard_map/ppermute | solution.py:21
  77.6 0.4 convolution_bitcast_fusion.7
  78.0 0.6 copy.17
  78.6 1.5 collective-permute-done.13
  80.1 1.9 %collective-permute-start.18 = (bf16[1,1,1,3,128,128]{5,3,4,2,1,0:T(4,128)(2,1)S(1)}, bf16[1,1,1,3,128,128]{5,3,4,2,1,0:T(4,128)(2,1)S(1)}, u32[]{:S(2)}, u32[]{:S(2)}) collective-permute-start(bf16[1,1,1,3,128,128]{5,3,4,2,1,0:T(4,128)(2,1)S(1)} %collective-permute-done.13), channel_id=1, source_target_pairs={{0,3},{1,0},{2,1},{3,2},{4,7},{5,4},{6,5},{7,6},{8,11},{9,8},{10,9... | collective-permute-start | bytes 294920 | tf_op jit(solution)/shard_map/ppermute | solution.py:21
  81.9 0.3 broadcast_select_fusion
  82.3 0.9 collective-permute-start.1
  83.1 0.4 convolution_bitcast_fusion.6
  83.6 0.6 copy.19
  84.2 0.3 collective-permute-done.18
  84.5 1.9 %collective-permute-start.23 = (bf16[1,1,1,3,128,128]{5,3,4,2,1,0:T(4,128)(2,1)S(1)}, bf16[1,1,1,3,128,128]{5,3,4,2,1,0:T(4,128)(2,1)S(1)}, u32[]{:S(2)}, u32[]{:S(2)}) collective-permute-start(bf16[1,1,1,3,128,128]{5,3,4,2,1,0:T(4,128)(2,1)S(1)} %collective-permute-done.18), channel_id=1, source_target_pairs={{0,3},{1,0},{2,1},{3,2},{4,7},{5,4},{6,5},{7,6},{8,11},{9,8},{10,9... | collective-permute-start | bytes 294920 | tf_op jit(solution)/shard_map/ppermute | solution.py:21
  86.3 0.4 convolution_bitcast_fusion.5
  86.8 0.6 copy.21
  87.3 1.5 collective-permute-done.23
  88.9 0.4 convolution_bitcast_fusion.4
  89.3 0.6 copy.23
  89.9 18.4 %collective-permute-done.1 = bf16[1,1,16,128,128]{4,2,3,1,0:T(8,128)(2,1)} collective-permute-done((bf16[1,1,16,128,128]{4,2,3,1,0:T(8,128)(2,1)S(1)}, bf16[1,1,16,128,128]{4,2,3,1,0:T(8,128)(2,1)}, u32[]{:S(2)}, u32[]{:S(2)}) %collective-permute-start.1) | collective-permute-done | bytes 524320 | tf_op jit(solution)/shard_map/ppermute | solution.py:21
  108.3 1.8 %collective-permute-start.10 = (bf16[1,1,16,128,128]{4,2,3,1,0:T(8,128)(2,1)S(1)}, bf16[1,1,16,128,128]{4,2,3,1,0:T(8,128)(2,1)S(1)}, u32[]{:S(2)}, u32[]{:S(2)}) collective-permute-start(bf16[1,1,16,128,128]{4,2,3,1,0:T(8,128)(2,1)S(1)} %broadcast_select_fusion.1), channel_id=1, source_target_pairs={{0,12},{4,0},{8,4},{12,8},{1,13},{5,1},{9,5},{13,9},{2,14},{6,2},{... | collective-permute-start | bytes 1572872 | tf_op jit(solution)/shard_map/ppermute | solution.py:21
  110.1 0.4 convolution_bitcast_fusion.3
  110.7 0.5 fusion.8
  111.2 10.3 %collective-permute-done.10 = bf16[1,1,16,128,128]{4,2,3,1,0:T(8,128)(2,1)S(1)} collective-permute-done((bf16[1,1,16,128,128]{4,2,3,1,0:T(8,128)(2,1)S(1)}, bf16[1,1,16,128,128]{4,2,3,1,0:T(8,128)(2,1)S(1)}, u32[]{:S(2)}, u32[]{:S(2)}) %collective-permute-start.10) | collective-permute-done | bytes 524320 | tf_op jit(solution)/shard_map/ppermute | solution.py:21
  121.5 4.3 %collective-permute-start.15 = (bf16[1,1,16,128,128]{4,2,3,1,0:T(8,128)(2,1)S(1)}, bf16[1,1,16,128,128]{4,2,3,1,0:T(8,128)(2,1)S(1)}, u32[]{:S(2)}, u32[]{:S(2)}) collective-permute-start(bf16[1,1,16,128,128]{4,2,3,1,0:T(8,128)(2,1)S(1)} %collective-permute-done.10), channel_id=1, source_target_pairs={{0,12},{4,0},{8,4},{12,8},{1,13},{5,1},{9,5},{13,9},{2,14},{6,2},{... | collective-permute-start | bytes 1572872 | tf_op jit(solution)/shard_map/ppermute | solution.py:21
  125.8 0.4 convolution_bitcast_fusion.2
  126.3 0.5 convolution_add_fusion.2
  126.8 9.4 %collective-permute-done.15 = bf16[1,1,16,128,128]{4,2,3,1,0:T(8,128)(2,1)S(1)} collective-permute-done((bf16[1,1,16,128,128]{4,2,3,1,0:T(8,128)(2,1)S(1)}, bf16[1,1,16,128,128]{4,2,3,1,0:T(8,128)(2,1)S(1)}, u32[]{:S(2)}, u32[]{:S(2)}) %collective-permute-start.15) | collective-permute-done | bytes 524320 | tf_op jit(solution)/shard_map/ppermute | solution.py:21
  136.3 4.3 %collective-permute-start.20 = (bf16[1,1,16,128,128]{4,2,3,1,0:T(8,128)(2,1)S(1)}, bf16[1,1,16,128,128]{4,2,3,1,0:T(8,128)(2,1)S(1)}, u32[]{:S(2)}, u32[]{:S(2)}) collective-permute-start(bf16[1,1,16,128,128]{4,2,3,1,0:T(8,128)(2,1)S(1)} %collective-permute-done.15), channel_id=1, source_target_pairs={{0,12},{4,0},{8,4},{12,8},{1,13},{5,1},{9,5},{13,9},{2,14},{6,2},{... | collective-permute-start | bytes 1572872 | tf_op jit(solution)/shard_map/ppermute | solution.py:21
  140.5 0.4 convolution_bitcast_fusion.1
  141.1 0.5 convolution_add_fusion.1
  141.6 8.5 %collective-permute-done.20 = bf16[1,1,16,128,128]{4,2,3,1,0:T(8,128)(2,1)S(1)} collective-permute-done((bf16[1,1,16,128,128]{4,2,3,1,0:T(8,128)(2,1)S(1)}, bf16[1,1,16,128,128]{4,2,3,1,0:T(8,128)(2,1)S(1)}, u32[]{:S(2)}, u32[]{:S(2)}) %collective-permute-start.20) | collective-permute-done | bytes 524320 | tf_op jit(solution)/shard_map/ppermute | solution.py:21
  150.1 0.4 convolution_bitcast_fusion
  151.0 1.2 fusion.1
  (50 shorter events, 1.8 us)
Async XLA Ops:
  0.0 7.0 %copy-start.3 = (s32[1,1,2,16]{3,2,1,0:T(2,128)S(1)}, s32[1,1,2,16]{3,2,1,0:T(2,128)}, u32[]{:S(2)}) copy-start(s32[1,1,2,16]{3,2,1,0:T(2,128)} %param.7) | copy-start | bytes 388
  0.0 7.4 %copy-start.1 = (bf16[1,1,1,3,128,128]{5,4,3,2,1,0:T(8,128)(2,1)S(1)}, bf16[1,1,1,3,128,128]{5,4,3,2,1,0:T(8,128)(2,1)}, u32[]{:S(2)}) copy-start(bf16[1,1,1,3,128,128]{5,4,3,2,1,0:T(8,128)(2,1)} %param.9) | copy-start | bytes 294916
  1.4 6.3 %copy-start.2 = (s32[1,1,1,2,3]{4,3,2,1,0:T(2,128)S(1)}, s32[1,1,1,2,3]{4,3,2,1,0:T(2,128)}, u32[]{:S(2)}) copy-start(s32[1,1,1,2,3]{4,3,2,1,0:T(2,128)} %param.10) | copy-start | bytes 76
  1.4 80.5 %collective-permute-start = (bf16[1,1,16,128,128]{4,2,3,1,0:T(8,128)(2,1)S(1)}, bf16[1,1,16,128,128]{4,2,3,1,0:T(8,128)(2,1)S(1)}, u32[]{:S(2)}, u32[]{:S(2)}) collective-permute-start(bf16[1,1,16,128,128]{4,2,3,1,0:T(8,128)(2,1)S(1)} %copy.12), channel_id=1, source_target_pairs={{0,12},{4,0},{8,4},{12,8},{1,13},{5,1},{9,5},{13,9},{2,14},{6,2},{... | collective-permute-start | bytes 1572872 | tf_op jit(solution)/shard_map/ppermute | solution.py:21
  6.5 11.2 %collective-permute-start.4 = (s32[1,1]{1,0:T(1,128)}, s32[1,1]{1,0:T(1,128)}, u32[]{:S(2)}, u32[]{:S(2)}) collective-permute-start(s32[1,1]{1,0:T(1,128)} %param.8), channel_id=1, source_target_pairs={{0,12},{4,0},{8,4},{12,8},{1,13},{5,1},{9,5},{13,9},{2,14},{6,2},{... | collective-permute-start | bytes 20 | tf_op jit(solution)/shard_map/ppermute | solution.py:21
  7.0 44.6 %collective-permute-start.2 = (s32[1,1,2,16]{3,2,1,0:T(2,128)S(1)}, s32[1,1,2,16]{3,2,1,0:T(2,128)S(1)}, u32[]{:S(2)}, u32[]{:S(2)}) collective-permute-start(s32[1,1,2,16]{3,2,1,0:T(2,128)S(1)} %copy-done.3), channel_id=1, source_target_pairs={{0,12},{4,0},{8,4},{12,8},{1,13},{5,1},{9,5},{13,9},{2,14},{6,2},{... | collective-permute-start | bytes 392 | tf_op jit(solution)/shard_map/ppermute | solution.py:21
  7.5 64.7 %collective-permute-start.6 = (bf16[1,1,1,3,128,128]{5,3,4,2,1,0:T(4,128)(2,1)S(1)}, bf16[1,1,1,3,128,128]{5,3,4,2,1,0:T(4,128)(2,1)S(1)}, u32[]{:S(2)}, u32[]{:S(2)}) collective-permute-start(bf16[1,1,1,3,128,128]{5,3,4,2,1,0:T(4,128)(2,1)S(1)} %copy.15), channel_id=1, source_target_pairs={{0,3},{1,0},{2,1},{3,2},{4,7},{5,4},{6,5},{7,6},{8,11},{9,8},{10,9... | collective-permute-start | bytes 294920 | tf_op jit(solution)/shard_map/ppermute | solution.py:21
  7.7 34.2 %collective-permute-start.8 = (s32[1,1,1,2,3]{4,3,2,1,0:T(2,128)S(1)}, s32[1,1,1,2,3]{4,3,2,1,0:T(2,128)S(1)}, u32[]{:S(2)}, u32[]{:S(2)}) collective-permute-start(s32[1,1,1,2,3]{4,3,2,1,0:T(2,128)S(1)} %copy-done.2), channel_id=1, source_target_pairs={{0,3},{1,0},{2,1},{3,2},{4,7},{5,4},{6,5},{7,6},{8,11},{9,8},{10,9... | collective-permute-start | bytes 80 | tf_op jit(solution)/shard_map/ppermute | solution.py:21
  9.9 0.7 copy-start.4
  18.4 4.5 %collective-permute-start.5 = (s32[1,1]{1,0:T(1,128)}, s32[1,1]{1,0:T(1,128)}, u32[]{:S(2)}, u32[]{:S(2)}) collective-permute-start(s32[1,1]{1,0:T(1,128)} %select_n.137), channel_id=1, source_target_pairs={{0,8},{4,12},{8,0},{12,4},{1,9},{5,13},{9,1},{13,5},{2,10},{6,14},... | collective-permute-start | bytes 20 | tf_op jit(solution)/shard_map/ppermute | solution.py:21
  23.5 5.6 %collective-permute-start.12 = (s32[1,1]{1,0:T(1,128)}, s32[1,1]{1,0:T(1,128)}, u32[]{:S(2)}, u32[]{:S(2)}) collective-permute-start(s32[1,1]{1,0:T(1,128)} %select_n.138), channel_id=1, source_target_pairs={{0,12},{4,0},{8,4},{12,8},{1,13},{5,1},{9,5},{13,9},{2,14},{6,2},{... | collective-permute-start | bytes 20 | tf_op jit(solution)/shard_map/ppermute | solution.py:21
  29.8 5.4 %collective-permute-start.17 = (s32[1,1]{1,0:T(1,128)}, s32[1,1]{1,0:T(1,128)}, u32[]{:S(2)}, u32[]{:S(2)}) collective-permute-start(s32[1,1]{1,0:T(1,128)} %collective-permute-done.12), channel_id=1, source_target_pairs={{0,12},{4,0},{8,4},{12,8},{1,13},{5,1},{9,5},{13,9},{2,14},{6,2},{... | collective-permute-start | bytes 20 | tf_op jit(solution)/shard_map/ppermute | solution.py:21
  35.8 5.4 %collective-permute-start.22 = (s32[1,1]{1,0:T(1,128)}, s32[1,1]{1,0:T(1,128)}, u32[]{:S(2)}, u32[]{:S(2)}) collective-permute-start(s32[1,1]{1,0:T(1,128)} %collective-permute-done.17), channel_id=1, source_target_pairs={{0,12},{4,0},{8,4},{12,8},{1,13},{5,1},{9,5},{13,9},{2,14},{6,2},{... | collective-permute-start | bytes 20 | tf_op jit(solution)/shard_map/ppermute | solution.py:21
  41.9 3.6 %collective-permute-start.9 = (s32[1,1,1,2,3]{4,3,2,1,0:T(2,128)S(1)}, s32[1,1,1,2,3]{4,3,2,1,0:T(2,128)S(1)}, u32[]{:S(2)}, u32[]{:S(2)}) collective-permute-start(s32[1,1,1,2,3]{4,3,2,1,0:T(2,128)S(1)} %broadcast_select_fusion.4), channel_id=1, source_target_pairs={{0,2},{1,3},{2,0},{3,1},{4,6},{5,7},{6,4},{7,5},{8,10},{9,11},{10,... | collective-permute-start | bytes 80 | tf_op jit(solution)/shard_map/ppermute | solution.py:21
  45.5 1.4 collective-permute-start.14
  46.9 3.0 %collective-permute-start.19 = (s32[1,1,1,2,3]{4,3,2,1,0:T(2,128)S(1)}, s32[1,1,1,2,3]{4,3,2,1,0:T(2,128)S(1)}, u32[]{:S(2)}, u32[]{:S(2)}) collective-permute-start(s32[1,1,1,2,3]{4,3,2,1,0:T(2,128)S(1)} %collective-permute-done.14), channel_id=1, source_target_pairs={{0,3},{1,0},{2,1},{3,2},{4,7},{5,4},{6,5},{7,6},{8,11},{9,8},{10,9... | collective-permute-start | bytes 80 | tf_op jit(solution)/shard_map/ppermute | solution.py:21
  49.9 3.0 %collective-permute-start.24 = (s32[1,1,1,2,3]{4,3,2,1,0:T(2,128)S(1)}, s32[1,1,1,2,3]{4,3,2,1,0:T(2,128)S(1)}, u32[]{:S(2)}, u32[]{:S(2)}) collective-permute-start(s32[1,1,1,2,3]{4,3,2,1,0:T(2,128)S(1)} %collective-permute-done.19), channel_id=1, source_target_pairs={{0,3},{1,0},{2,1},{3,2},{4,7},{5,4},{6,5},{7,6},{8,11},{9,8},{10,9... | collective-permute-start | bytes 80 | tf_op jit(solution)/shard_map/ppermute | solution.py:21
  51.6 4.5 %collective-permute-start.3 = (s32[1,1,2,16]{3,2,1,0:T(2,128)S(1)}, s32[1,1,2,16]{3,2,1,0:T(2,128)S(1)}, u32[]{:S(2)}, u32[]{:S(2)}) collective-permute-start(s32[1,1,2,16]{3,2,1,0:T(2,128)S(1)} %broadcast_select_fusion.6), channel_id=1, source_target_pairs={{0,8},{4,12},{8,0},{12,4},{1,9},{5,13},{9,1},{13,5},{2,10},{6,14},... | collective-permute-start | bytes 392 | tf_op jit(solution)/shard_map/ppermute | solution.py:21
  56.0 5.3 %collective-permute-start.11 = (s32[1,1,2,16]{3,2,1,0:T(2,128)S(1)}, s32[1,1,2,16]{3,2,1,0:T(2,128)S(1)}, u32[]{:S(2)}, u32[]{:S(2)}) collective-permute-start(s32[1,1,2,16]{3,2,1,0:T(2,128)S(1)} %broadcast_select_fusion.7), channel_id=1, source_target_pairs={{0,12},{4,0},{8,4},{12,8},{1,13},{5,1},{9,5},{13,9},{2,14},{6,2},{... | collective-permute-start | bytes 392 | tf_op jit(solution)/shard_map/ppermute | solution.py:21
  61.4 5.4 %collective-permute-start.16 = (s32[1,1,2,16]{3,2,1,0:T(2,128)S(1)}, s32[1,1,2,16]{3,2,1,0:T(2,128)S(1)}, u32[]{:S(2)}, u32[]{:S(2)}) collective-permute-start(s32[1,1,2,16]{3,2,1,0:T(2,128)S(1)} %collective-permute-done.11), channel_id=1, source_target_pairs={{0,12},{4,0},{8,4},{12,8},{1,13},{5,1},{9,5},{13,9},{2,14},{6,2},{... | collective-permute-start | bytes 392 | tf_op jit(solution)/shard_map/ppermute | solution.py:21
  66.8 5.4 %collective-permute-start.21 = (s32[1,1,2,16]{3,2,1,0:T(2,128)S(1)}, s32[1,1,2,16]{3,2,1,0:T(2,128)S(1)}, u32[]{:S(2)}, u32[]{:S(2)}) collective-permute-start(s32[1,1,2,16]{3,2,1,0:T(2,128)S(1)} %collective-permute-done.16), channel_id=1, source_target_pairs={{0,12},{4,0},{8,4},{12,8},{1,13},{5,1},{9,5},{13,9},{2,14},{6,2},{... | collective-permute-start | bytes 392 | tf_op jit(solution)/shard_map/ppermute | solution.py:21
  72.4 5.0 %collective-permute-start.7 = (bf16[1,1,1,3,128,128]{5,3,4,2,1,0:T(4,128)(2,1)S(1)}, bf16[1,1,1,3,128,128]{5,3,4,2,1,0:T(4,128)(2,1)S(1)}, u32[]{:S(2)}, u32[]{:S(2)}) collective-permute-start(bf16[1,1,1,3,128,128]{5,3,4,2,1,0:T(4,128)(2,1)S(1)} %broadcast_select_fusion.2), channel_id=1, source_target_pairs={{0,2},{1,3},{2,0},{3,1},{4,6},{5,7},{6,4},{7,5},{8,10},{9,11},{10,... | collective-permute-start | bytes 294920 | tf_op jit(solution)/shard_map/ppermute | solution.py:21
  77.5 2.6 %collective-permute-start.13 = (bf16[1,1,1,3,128,128]{5,3,4,2,1,0:T(4,128)(2,1)S(1)}, bf16[1,1,1,3,128,128]{5,3,4,2,1,0:T(4,128)(2,1)S(1)}, u32[]{:S(2)}, u32[]{:S(2)}) collective-permute-start(bf16[1,1,1,3,128,128]{5,3,4,2,1,0:T(4,128)(2,1)S(1)} %broadcast_select_fusion.3), channel_id=1, source_target_pairs={{0,3},{1,0},{2,1},{3,2},{4,7},{5,4},{6,5},{7,6},{8,11},{9,8},{10,9... | collective-permute-start | bytes 294920 | tf_op jit(solution)/shard_map/ppermute | solution.py:21
  78.0 4.0 %copy-start = (bf16[1,1,16,128,128]{4,3,2,1,0:T(8,128)(2,1)S(1)}, bf16[1,1,16,128,128]{4,3,2,1,0:T(8,128)(2,1)}, u32[]{:S(2)}) copy-start(bf16[1,1,16,128,128]{4,3,2,1,0:T(8,128)(2,1)} %param.6) | copy-start | bytes 1572868
  80.1 4.4 %collective-permute-start.18 = (bf16[1,1,1,3,128,128]{5,3,4,2,1,0:T(4,128)(2,1)S(1)}, bf16[1,1,1,3,128,128]{5,3,4,2,1,0:T(4,128)(2,1)S(1)}, u32[]{:S(2)}, u32[]{:S(2)}) collective-permute-start(bf16[1,1,1,3,128,128]{5,3,4,2,1,0:T(4,128)(2,1)S(1)} %collective-permute-done.13), channel_id=1, source_target_pairs={{0,3},{1,0},{2,1},{3,2},{4,7},{5,4},{6,5},{7,6},{8,11},{9,8},{10,9... | collective-permute-start | bytes 294920 | tf_op jit(solution)/shard_map/ppermute | solution.py:21
  82.3 26.0 %collective-permute-start.1 = (bf16[1,1,16,128,128]{4,2,3,1,0:T(8,128)(2,1)S(1)}, bf16[1,1,16,128,128]{4,2,3,1,0:T(8,128)(2,1)}, u32[]{:S(2)}, u32[]{:S(2)}) collective-permute-start(bf16[1,1,16,128,128]{4,2,3,1,0:T(8,128)(2,1)S(1)} %broadcast_select_fusion), channel_id=1, source_target_pairs={{0,8},{4,12},{8,0},{12,4},{1,9},{5,13},{9,1},{13,5},{2,10},{6,14},... | collective-permute-start | bytes 1572872 | tf_op jit(solution)/shard_map/ppermute | solution.py:21
  84.5 4.4 %collective-permute-start.23 = (bf16[1,1,1,3,128,128]{5,3,4,2,1,0:T(4,128)(2,1)S(1)}, bf16[1,1,1,3,128,128]{5,3,4,2,1,0:T(4,128)(2,1)S(1)}, u32[]{:S(2)}, u32[]{:S(2)}) collective-permute-start(bf16[1,1,1,3,128,128]{5,3,4,2,1,0:T(4,128)(2,1)S(1)} %collective-permute-done.18), channel_id=1, source_target_pairs={{0,3},{1,0},{2,1},{3,2},{4,7},{5,4},{6,5},{7,6},{8,11},{9,8},{10,9... | collective-permute-start | bytes 294920 | tf_op jit(solution)/shard_map/ppermute | solution.py:21
  108.3 13.1 %collective-permute-start.10 = (bf16[1,1,16,128,128]{4,2,3,1,0:T(8,128)(2,1)S(1)}, bf16[1,1,16,128,128]{4,2,3,1,0:T(8,128)(2,1)S(1)}, u32[]{:S(2)}, u32[]{:S(2)}) collective-permute-start(bf16[1,1,16,128,128]{4,2,3,1,0:T(8,128)(2,1)S(1)} %broadcast_select_fusion.1), channel_id=1, source_target_pairs={{0,12},{4,0},{8,4},{12,8},{1,13},{5,1},{9,5},{13,9},{2,14},{6,2},{... | collective-permute-start | bytes 1572872 | tf_op jit(solution)/shard_map/ppermute | solution.py:21
  121.5 14.8 %collective-permute-start.15 = (bf16[1,1,16,128,128]{4,2,3,1,0:T(8,128)(2,1)S(1)}, bf16[1,1,16,128,128]{4,2,3,1,0:T(8,128)(2,1)S(1)}, u32[]{:S(2)}, u32[]{:S(2)}) collective-permute-start(bf16[1,1,16,128,128]{4,2,3,1,0:T(8,128)(2,1)S(1)} %collective-permute-done.10), channel_id=1, source_target_pairs={{0,12},{4,0},{8,4},{12,8},{1,13},{5,1},{9,5},{13,9},{2,14},{6,2},{... | collective-permute-start | bytes 1572872 | tf_op jit(solution)/shard_map/ppermute | solution.py:21
  136.3 13.9 %collective-permute-start.20 = (bf16[1,1,16,128,128]{4,2,3,1,0:T(8,128)(2,1)S(1)}, bf16[1,1,16,128,128]{4,2,3,1,0:T(8,128)(2,1)S(1)}, u32[]{:S(2)}, u32[]{:S(2)}) collective-permute-start(bf16[1,1,16,128,128]{4,2,3,1,0:T(8,128)(2,1)S(1)} %collective-permute-done.15), channel_id=1, source_target_pairs={{0,12},{4,0},{8,4},{12,8},{1,13},{5,1},{9,5},{13,9},{2,14},{6,2},{... | collective-permute-start | bytes 1572872 | tf_op jit(solution)/shard_map/ppermute | solution.py:21
where the time goes:
time: 152 us
  waiting for transfers between devices  77.1 us (51%)
  starting transfers between devices  58.8 us (39%)
  matrix products  5.88 us (4%)
  local copies, waits for them, and re-layouts  5.59 us (4%)
  other arithmetic  2.54 us (2%)
  between operations  2.31 us (2%)
    ppermute x25, waiting for transfers between devices, passed_along(): return lax.ppermute(value, axis, pairs)  77.1 us
    ppermute x25, starting transfers between devices, passed_along(): return lax.ppermute(value, axis, pairs)  58.8 us
  transfers between devices with their start and end apart: 25, of which 20 were waited for; matrix products, arithmetic and copies ran while one was open for 6% of the time, Pallas kernels for 0%

commit v1 on v0

--- a/solution.py
+++ b/solution.py
@@ -1,6 +1,8 @@
 import jax
 import jax.numpy as jnp
 from jax import lax
+from jax.experimental import pallas as pl
+from jax.experimental.pallas import tpu as pltpu
 from jax.sharding import PartitionSpec as P
 
 BS = 128
@@ -105,6 +107,354 @@
     return filtered.reshape(MR * BS, NC * BS).astype(jnp.bfloat16)
 
 
+CHUNKS = (32, 32, 32, 32)
+STARTS = tuple(sum(CHUNKS[:n]) for n in range(len(CHUNKS)))
+NCH = len(CHUNKS)
+ZERO = NZA
+B_INNER = 64
+B_COLUMN = 72
+DEPTH = NZB * BS
+WIDE = NC * BS
+
+
+def line_kernel(
+    a_index, a_live, b_index, c_keep, a_ref, b_ref, o_ref,
+    own_a, inner_a, outer_a, far_0, far_1, far_2, far_3,
+    own_b, outer_b, own_w, outer_w, own_sum, outer_sum, sum_in,
+    own_tab, inner_tab, outer_tab, far_tab, own_bt, outer_bt,
+    own_st, inner_st, outer_st, far_st, own_bs, outer_bs,
+    local_sem, smem_sem, a_send, a_recv, tab_send, tab_recv,
+    b_send, b_recv, bt_send, bt_recv, sum_send, sum_recv,
+):
+    far_a = (far_0, far_1, far_2, far_3)
+    row = lax.axis_index("row")
+    col = lax.axis_index("col")
+    is_end = jnp.logical_or(row == 0, row == 3)
+    is_middle = jnp.logical_not(is_end)
+    outer = jnp.where(row == 1, 0, 3)
+    inner = 3 - row
+    beside = jnp.where(row == 0, 1, 2)
+    panels = (row, inner, 3 - outer, outer)
+
+    def to_row(src, dst, send, recv, target):
+        return pltpu.make_async_remote_copy(
+            src_ref=src, dst_ref=dst, send_sem=send, recv_sem=recv,
+            device_id={"row": target}, device_id_type=pl.DeviceIdType.MESH,
+        )
+
+    def to_col(src, dst, send, recv, target):
+        return pltpu.make_async_remote_copy(
+            src_ref=src, dst_ref=dst, send_sem=send, recv_sem=recv,
+            device_id={"col": target}, device_id_type=pl.DeviceIdType.MESH,
+        )
+
+    def others():
+        return [lax.rem(col + step, 4) for step in range(1, 4)]
+
+    blocks = pl.ds(0, NZA)
+    copy_a = pltpu.make_async_copy(a_ref.at[0, 0], own_a.at[blocks], local_sem.at[0])
+    copy_b = pltpu.make_async_copy(b_ref.at[0, 0, 0], own_b.at[col], local_sem.at[1])
+    copy_a.start()
+    copy_b.start()
+
+    lane = lax.broadcasted_iota(jnp.int32, (8, BS), 1)
+    table = jnp.full((8, BS), ZERO, jnp.int32)
+    live = a_live[0, 0]
+    for slot in range(NZA):
+        place = a_index[0, 0, 0, slot] * KP + a_index[0, 0, 1, slot]
+        place = jnp.where(slot < live, place, -1)
+        table = jnp.where(lane == place, slot, table)
+    for slot in range(NZB):
+        table = jnp.where(lane == B_INNER + slot, b_index[0, 0, 0, 0, slot], table)
+        table = jnp.where(lane == B_COLUMN + slot, b_index[0, 0, 0, 1, slot], table)
+    own_tab[...] = table
+    own_bt[col] = table
+    blank = jnp.zeros((BS, BS), jnp.bfloat16)
+    own_a[ZERO] = blank
+    inner_a[ZERO] = blank
+    outer_a[ZERO] = blank
+    for n in range(NCH):
+        far_a[n][ZERO] = blank[: CHUNKS[n]]
+
+    barrier = pltpu.get_barrier_semaphore()
+    for target in others():
+        pl.semaphore_signal(
+            barrier, inc=1, device_id={"col": target}, device_id_type=pl.DeviceIdType.MESH
+        )
+
+    @pl.when(is_end)
+    def _():
+        pl.semaphore_signal(
+            barrier, inc=1, device_id={"row": beside}, device_id_type=pl.DeviceIdType.MESH
+        )
+        pl.semaphore_wait(barrier, 4)
+
+    @pl.when(is_middle)
+    def _():
+        for target in (outer, inner):
+            pl.semaphore_signal(
+                barrier, inc=1, device_id={"row": target}, device_id_type=pl.DeviceIdType.MESH
+            )
+        pl.semaphore_wait(barrier, 5)
+
+    def to_smem(src, dst, n):
+        return pltpu.make_async_copy(src, dst, smem_sem.at[n])
+
+    def place_b(w_ref, at, blocks_ref, meta, panel):
+        for slot in range(NZB):
+            column = meta[panel, 0, B_COLUMN + slot]
+            block = blocks_ref[panel, slot].astype(jnp.float32)
+            for c in range(NC):
+                hot = jnp.where(column == c, 1.0, 0.0)
+                w_ref[pl.ds(at * DEPTH + slot * BS, BS), pl.ds(c * BS, BS)] = (
+                    block * hot
+                ).astype(jnp.bfloat16)
+
+    def picked(a_buf, tab, meta, panel, r):
+        return jnp.concatenate(
+            [a_buf[tab[0, r * KP + meta[panel, 0, B_INNER + slot]]] for slot in range(NZB)],
+            axis=1,
+        )
+
+    def times(x, w_ref, at):
+        return jnp.dot(
+            x, w_ref[pl.ds(at * DEPTH, DEPTH), :], preferred_element_type=jnp.float32
+        )
+
+    def store(r, start, size, value):
+        for c in range(NC):
+            kept = value[:, c * BS : (c + 1) * BS] * c_keep[r, c].astype(jnp.float32)
+            o_ref[pl.ds(r * BS + start, size), pl.ds(c * BS, BS)] = kept.astype(jnp.bfloat16)
+
+    @pl.when(is_end)
+    def _():
+        sends = [
+            to_row(own_tab, outer_tab, tab_send.at[0], tab_recv.at[0], beside),
+            to_row(own_bt.at[col], outer_bt.at[col], tab_send.at[1], bt_recv.at[1, col], beside),
+            to_row(b_ref.at[0, 0, 0], outer_b.at[col], b_send.at[0, 0], b_recv.at[1, col], beside),
+        ]
+        for n in range(NCH):
+            piece = pl.ds(STARTS[n], CHUNKS[n])
+            sends.append(
+                to_row(
+                    a_ref.at[0, 0, :, piece, :], outer_a.at[blocks, piece, :],
+                    a_send.at[n], a_recv.at[n], beside,
+                )
+            )
+        for send in sends:
+            send.start()
+
+        def shared():
+            out = []
+            for n, target in enumerate(others()):
+                out.append(
+                    to_col(b_ref.at[0, 0, 0], own_b.at[col], b_send.at[1, n], b_recv.at[0, col], target)
+                )
+                out.append(
+                    to_col(own_tab, own_bt.at[col], bt_send.at[0, n], bt_recv.at[0, col], target)
+                )
+            return out
+
+        @pl.when(col == row)
+        def _():
+            for send in shared():
+                send.start()
+
+        @pl.when(col != row)
+        def _():
+            to_col(own_bt.at[row], own_bt.at[row], bt_send.at[0, 0], bt_recv.at[0, row], col).wait_recv()
+            to_col(own_b.at[row], own_b.at[row], b_send.at[1, 0], b_recv.at[0, row], col).wait_recv()
+
+        loads = [to_smem(own_tab, own_st, 0), to_smem(own_bt, own_bs, 1)]
+        for load in loads:
+            load.start()
+        copy_a.wait()
+        copy_b.wait()
+        for load in loads:
+            load.wait()
+        place_b(own_w, 0, own_b, own_bs, row)
+
+        def own_part(r, carry):
+            own_sum[r] = times(picked(own_a, own_st, own_bs, row, r), own_w, 0)
+            return carry
+
+        lax.fori_loop(0, MR, own_part, 0)
+        for n in range(NCH):
+            piece = pl.ds(STARTS[n], CHUNKS[n])
+            to_row(
+                sum_in.at[:, piece, :], sum_in.at[:, piece, :],
+                sum_send.at[n], sum_recv.at[n], beside,
+            ).wait_recv()
+            for r in range(MR):
+                store(r, STARTS[n], CHUNKS[n], own_sum[r, piece, :] + sum_in[r, piece, :])
+        for send in sends:
+            send.wait_send()
+
+        @pl.when(col == row)
+        def _():
+            for send in shared():
+                send.wait_send()
+
+    @pl.when(is_middle)
+    def _():
+        sends = [
+            to_row(own_tab, inner_tab, tab_send.at[0], tab_recv.at[1], inner),
+            to_row(a_ref.at[0, 0], inner_a.at[blocks], a_send.at[NCH], a_recv.at[NCH], inner),
+        ]
+        for n, target in enumerate(others()):
+            sends.append(
+                to_col(own_tab, own_bt.at[col], bt_send.at[0, n], bt_recv.at[0, col], target)
+            )
+            sends.append(
+                to_col(b_ref.at[0, 0, 0], own_b.at[col], b_send.at[0, n], b_recv.at[0, col], target)
+            )
+        for send in sends:
+            send.start()
+
+        to_row(outer_tab, outer_tab, tab_send.at[1], tab_recv.at[0], outer).wait_recv()
+        onward = [to_row(outer_tab, far_tab, tab_send.at[1], tab_recv.at[2], inner)]
+        onward[0].start()
+
+        def passed_b():
+            out = []
+            for n, target in enumerate(others()):
+                out.append(
+                    to_col(outer_bt.at[col], outer_bt.at[col], bt_send.at[1, n], bt_recv.at[1, col], target)
+                )
+                out.append(
+                    to_col(outer_b.at[col], outer_b.at[col], b_send.at[1, n], b_recv.at[1, col], target)
+                )
+            return out
+
+        to_row(outer_bt.at[col], outer_bt.at[col], tab_send.at[1], bt_recv.at[1, col], outer).wait_recv()
+        to_row(outer_b.at[col], outer_b.at[col], tab_send.at[1], b_recv.at[1, col], outer).wait_recv()
+
+        @pl.when(col != outer)
+        def _():
+            for send in passed_b():
+                send.start()
+
+        for n in range(NCH):
+            piece = pl.ds(STARTS[n], CHUNKS[n])
+            part = outer_a.at[blocks, piece, :]
+            to_row(part, part, a_send.at[n], a_recv.at[n], outer).wait_recv()
+            send = to_row(part, far_a[n].at[blocks], a_send.at[n], a_recv.at[NCH + 1 + n], inner)
+            send.start()
+            onward.append(send)
+
+        for source in others():
+            to_col(own_bt.at[source], own_bt.at[source], bt_send.at[0, 0], bt_recv.at[0, source], col).wait_recv()
+            to_col(own_b.at[source], own_b.at[source], b_send.at[0, 0], b_recv.at[0, source], col).wait_recv()
+
+            @pl.when(source != outer)
+            def _():
+                to_col(outer_bt.at[source], outer_bt.at[source], bt_send.at[0, 0], bt_recv.at[1, source], col).wait_recv()
+                to_col(outer_b.at[source], outer_b.at[source], b_send.at[0, 0], b_recv.at[1, source], col).wait_recv()
+
+        to_row(inner_tab, inner_tab, tab_send.at[1], tab_recv.at[1], inner).wait_recv()
+        to_row(far_tab, far_tab, tab_send.at[1], tab_recv.at[2], inner).wait_recv()
+        loads = [
+            to_smem(src, dst, n)
+            for n, (src, dst) in enumerate(
+                (
+                    (own_tab, own_st), (inner_tab, inner_st), (outer_tab, outer_st),
+                    (far_tab, far_st), (own_bt, own_bs), (outer_bt, outer_bs),
+                )
+            )
+        ]
+        for load in loads:
+            load.start()
+        copy_a.wait()
+        copy_b.wait()
+        for load in loads:
+            load.wait()
+        for at, panel in enumerate(panels):
+            place_b(own_w, at, own_b, own_bs, panel)
+            if at < 3:
+                place_b(outer_w, at, outer_b, outer_bs, panel)
+
+        def own_part(r, carry):
+            own_sum[r] = times(
+                picked(own_a, own_st, own_bs, panels[0], r), own_w, 0
+            ) + times(picked(outer_a, outer_st, own_bs, panels[3], r), own_w, 3)
+            outer_sum[r] = times(picked(own_a, own_st, outer_bs, panels[0], r), outer_w, 0)
+            return carry
+
+        lax.fori_loop(0, MR, own_part, 0)
+        to_row(
+            inner_a.at[blocks], inner_a.at[blocks], a_send.at[0], a_recv.at[NCH], inner
+        ).wait_recv()
+
+        def inner_part(r, carry):
+            own_sum[r] += times(picked(inner_a, inner_st, own_bs, panels[1], r), own_w, 1)
+            outer_sum[r] += times(picked(inner_a, inner_st, outer_bs, panels[1], r), outer_w, 1)
+            return carry
+
+        lax.fori_loop(0, MR, inner_part, 0)
+
+        def far_part(n, w_ref, meta):
+            x = jnp.concatenate(
+                [picked(far_a[n], far_st, meta, panels[2], r) for r in range(MR)], axis=0
+            )
+            return times(x, w_ref, 2).reshape(MR, CHUNKS[n], WIDE)
+
+        for n in range(NCH):
+            piece = pl.ds(STARTS[n], CHUNKS[n])
+            to_row(
+                far_a[n].at[blocks], far_a[n].at[blocks], a_send.at[0], a_recv.at[NCH + 1 + n], inner
+            ).wait_recv()
+            outer_sum[:, piece, :] += far_part(n, outer_w, outer_bs)
+            send = to_row(
+                outer_sum.at[:, piece, :], sum_in.at[:, piece, :],
+                sum_send.at[n], sum_recv.at[n], outer,
+            )
+            send.start()
+            onward.append(send)
+            mine = own_sum[:, piece, :] + far_part(n, own_w, own_bs)
+            for r in range(MR):
+                store(r, STARTS[n], CHUNKS[n], mine[r])
+        for send in sends + onward:
+            send.wait_send()
+
+        @pl.when(col != outer)
+        def _():
+            for send in passed_b():
+                send.wait_send()
+
+
+def line_local(a_blocks, a_index, a_live, b_blocks, b_index, c_keep):
+    scalar = pl.BlockSpec(memory_space=pltpu.SMEM)
+    anywhere = pl.BlockSpec(memory_space=pl.ANY)
+    dma = pltpu.SemaphoreType.DMA
+    panel = pltpu.VMEM((NZA + 1, BS, BS), jnp.bfloat16)
+    meta = (8, BS)
+    total = pltpu.VMEM((MR, BS, WIDE), jnp.float32)
+    return pl.pallas_call(
+        line_kernel,
+        out_shape=jax.ShapeDtypeStruct((MR * BS, WIDE), jnp.bfloat16),
+        in_specs=[scalar] * 4 + [anywhere] * 2,
+        out_specs=pl.BlockSpec(memory_space=pltpu.VMEM),
+        scratch_shapes=[panel] * 3
+        + [pltpu.VMEM((NZA + 1, size, BS), jnp.bfloat16) for size in CHUNKS]
+        + [pltpu.VMEM((4, NZB, BS, BS), jnp.bfloat16)] * 2
+        + [pltpu.VMEM((4 * DEPTH, WIDE), jnp.bfloat16), pltpu.VMEM((3 * DEPTH, WIDE), jnp.bfloat16)]
+        + [total] * 3
+        + [pltpu.VMEM(meta, jnp.int32)] * 4
+        + [pltpu.VMEM((4,) + meta, jnp.int32)] * 2
+        + [pltpu.SMEM(meta, jnp.int32)] * 4
+        + [pltpu.SMEM((4,) + meta, jnp.int32)] * 2
+        + [
+            dma((2,)), dma((6,)),
+            dma((NCH + 1,)), dma((2 * NCH + 1,)), dma((2,)), dma((3,)),
+            dma((2, 3)), dma((2, 4)), dma((2, 3)), dma((2, 4)),
+            dma((NCH,)), dma((NCH,)),
+        ],
+        compiler_params=pltpu.CompilerParams(
+            collective_id=0, has_side_effects=True, vmem_limit_bytes=32 * 1024 * 1024
+        ),
+    )(a_index, a_live, b_index, c_keep, a_blocks, b_blocks)
+
+
 def solution(mesh):
     placed = (
         P(("groups", "row"), "col", None, None, None),
@@ -114,6 +464,7 @@
         P(("groups", "row"), "col", None, None, None),
         P(("groups", "col"), "row"),
     )
+    short_line = mesh.shape["row"] == 4 and mesh.shape["col"] == 4
     return jax.shard_map(
-        local, mesh=mesh, in_specs=placed, out_specs=P(("groups", "col"), "row"), check_vma=False
+        line_local if short_line else local, mesh=mesh, in_specs=placed, out_specs=P(("groups", "col"), "row"), check_vma=False
     )

time: 152 us -> 40.5 us (0.27)
  waiting for transfers between devices: 77.1 us -> 0 us
  starting transfers between devices: 58.8 us -> 0 us
  Pallas kernels: 0 us -> 36.3 us
  matrix products: 5.88 us -> 0 us
  other arithmetic: 2.54 us -> 0 us
  local copies, waits for them, and re-layouts: 5.59 us -> 3.33 us
  between operations: 2.31 us -> 0.69 us
    ppermute x25 -> x0, waiting for transfers between devices: 77.1 us -> none  [passed_along(): return lax.ppermute(value, axis, pairs)]
    ppermute x25 -> x0, starting transfers between devices: 58.8 us -> none  [passed_along(): return lax.ppermute(value, axis, pairs)]
    pallas_call x0 -> x1, Pallas kernels: none -> 36.3 us  [line_local(): pl.pallas_call(line_kernel, out_shape=jax.ShapeDtypeStruct((MR * BS, WIDE...]
    dot_general x12 -> x0, matrix products: 5.88 us -> none  [the longest x4 2.61 us: panel_product(): return total + jnp.dot(dense_a, dense_b, preferred_element_type=jnp.float32)]
    transpose x8 -> x0, local copies, waits for them, and re-layouts: 3.08 us -> none  [the longest x4 2.35 us: panel_product(): jnp.einsum('kcz,zuv->kucv', picker, second_blocks, preferred_element_type...]
    convert_element_type x13 -> x0, other arithmetic: 1.94 us -> none  [the longest x4 1.89 us: panel_product(): (jnp.arange(NZA, dtype=jnp.int32) < first_live).astype(jnp.bfloat16)]
  transfers between devices with their start and end apart: 25 -> 0, of which waited for: 20 -> 0; matrix products, arithmetic and copies ran while one was open for 6% -> 0% of each run, Pallas kernels for 0% -> 0%
where the time goes in v1:
time: 40.5 us; the launch traced here: 40.3 us
  Pallas kernels  36.3 us (90%)
  local copies, waits for them, and re-layouts  3.33 us (8%)
  between operations  0.69 us (2%)
    pallas_call x1, Pallas kernels, line_local(): pl.pallas_call(line_kernel, out_shape=jax.ShapeDtypeStruct((MR * BS, WIDE...  36.3 us
    unnamed x12, local copies, waits for them, and re-layouts  3.33 us

profile of v1, /device:TPU:0, one launch (start us, length us, event | category | flops | bytes accessed | tf_op | source)
XLA Modules:
  0.0 40.3 jit_solution(16707610360763557469)
XLA Ops:
  0.0 0.0 copy-start.4
  0.7 0.0 copy-done.4
  0.7 0.0 copy-start.2
  0.7 0.0 copy-start.3
  0.7 0.1 copy.7.c_keep
  0.8 0.6 %copy-done.2 = s32[1,1,2,16]{3,2,1,0:T(2,128)S(1)} copy-done((s32[1,1,2,16]{3,2,1,0:T(2,128)S(1)}, s32[1,1,2,16]{3,2,1,0:T(2,128)}, u32[]{:S(2)}) %copy-start.2) | copy-done | bytes 152
  1.4 0.0 copy-done.3
  1.4 0.0 copy-start
  1.4 1.0 %copy-done = bf16[1,1,16,128,128]{4,3,2,1,0:T(8,128)(2,1)S(1)} copy-done((bf16[1,1,16,128,128]{4,3,2,1,0:T(8,128)(2,1)S(1)}, bf16[1,1,16,128,128]{4,3,2,1,0:T(8,128)(2,1)}, u32[]{:S(2)}) %copy-start) | copy-done | bytes 524312
  2.4 0.0 copy-start.1
  2.4 0.9 %copy-done.1 = bf16[1,1,1,3,128,128]{5,4,3,2,1,0:T(8,128)(2,1)S(1)} copy-done((bf16[1,1,1,3,128,128]{5,4,3,2,1,0:T(8,128)(2,1)S(1)}, bf16[1,1,1,3,128,128]{5,4,3,2,1,0:T(8,128)(2,1)}, u32[]{:S(2)}) %copy-start.1) | copy-done | bytes 98328
  3.3 36.3 %shard_map.64 = bf16[512,256]{1,0:T(8,128)(2,1)S(1)} custom-call(s32[1,1,2,16]{3,2,1,0:T(2,128)S(1)} %copy-done.2, s32[1,1]{1,0:T(1,128)S(6)} %copy.9.a_live, s32[1,1,1,2,3]{4,3,2,1,0:T(2,128)S(1)} %copy-done.3, s32[4,2]{1,0:T(4,128)S(1)} %copy.7.c_keep, bf16[1,1,16,128,128]{4,3,2,1,0:T(8,128)(2,1)S(1)} %copy-done, bf16[1,1,1,3,128,128]{5,4,3,2,1,0:T(8,128)(2,1)S(1)} %copy-done.1), custom_call_target="tpu_custom_call" | custom-call | tf_op jit(solution)/shard_map/pallas_call | solution.py:432
  39.6 0.7 %copy.10 = bf16[512,256]{1,0:T(8,128)(2,1)} copy(bf16[512,256]{1,0:T(8,128)(2,1)S(1)} %shard_map.64) | data formatting | bytes 524288
Async XLA Ops:
  0.0 0.7 %copy-start.4 = (s32[4,2]{0,1:T(2,128)S(1)}, s32[4,2]{0,1:T(2,128)}, u32[]{:S(2)}) copy-start(s32[4,2]{0,1:T(2,128)} %param.11) | copy-start | bytes 100
  0.7 0.7 %copy-start.2 = (s32[1,1,2,16]{3,2,1,0:T(2,128)S(1)}, s32[1,1,2,16]{3,2,1,0:T(2,128)}, u32[]{:S(2)}) copy-start(s32[1,1,2,16]{3,2,1,0:T(2,128)} %a_index.1) | copy-start | bytes 388
  0.7 0.7 %copy-start.3 = (s32[1,1,1,2,3]{4,3,2,1,0:T(2,128)S(1)}, s32[1,1,1,2,3]{4,3,2,1,0:T(2,128)}, u32[]{:S(2)}) copy-start(s32[1,1,1,2,3]{4,3,2,1,0:T(2,128)} %b_index.1) | copy-start | bytes 76
  1.4 1.0 %copy-start = (bf16[1,1,16,128,128]{4,3,2,1,0:T(8,128)(2,1)S(1)}, bf16[1,1,16,128,128]{4,3,2,1,0:T(8,128)(2,1)}, u32[]{:S(2)}) copy-start(bf16[1,1,16,128,128]{4,3,2,1,0:T(8,128)(2,1)} %a_ref.1) | copy-start | bytes 1572868
  2.4 0.9 %copy-start.1 = (bf16[1,1,1,3,128,128]{5,4,3,2,1,0:T(8,128)(2,1)S(1)}, bf16[1,1,1,3,128,128]{5,4,3,2,1,0:T(8,128)(2,1)}, u32[]{:S(2)}) copy-start(bf16[1,1,1,3,128,128]{5,4,3,2,1,0:T(8,128)(2,1)} %b_ref.1) | copy-start | bytes 294916

commit v2 on v1

--- a/solution.py
+++ b/solution.py
@@ -107,9 +107,12 @@
     return filtered.reshape(MR * BS, NC * BS).astype(jnp.bfloat16)
 
 
-CHUNKS = (32, 32, 32, 32)
+CHUNKS = (32,32,16,16,16,16)
 STARTS = tuple(sum(CHUNKS[:n]) for n in range(len(CHUNKS)))
 NCH = len(CHUNKS)
+EARLY = 8
+AHEAD = 3
+END_AHEAD = 2
 ZERO = NZA
 B_INNER = 64
 B_COLUMN = 72
@@ -118,15 +121,14 @@
 
 
 def line_kernel(
-    a_index, a_live, b_index, c_keep, a_ref, b_ref, o_ref,
-    own_a, inner_a, outer_a, far_0, far_1, far_2, far_3,
-    own_b, outer_b, own_w, outer_w, own_sum, outer_sum, sum_in,
+    a_index_in, a_live_in, b_index_in, c_keep_in, a_ref, b_ref, o_ref,
+    own_a, outer_a, inner_a, far_a, own_b, outer_b, own_w, outer_w, own_sum, outer_sum, sum_in,
     own_tab, inner_tab, outer_tab, far_tab, own_bt, outer_bt,
     own_st, inner_st, outer_st, far_st, own_bs, outer_bs,
     local_sem, smem_sem, a_send, a_recv, tab_send, tab_recv,
     b_send, b_recv, bt_send, bt_recv, sum_send, sum_recv,
+    a_index, a_live, b_index, c_keep, in_sem,
 ):
-    far_a = (far_0, far_1, far_2, far_3)
     row = lax.axis_index("row")
     col = lax.axis_index("col")
     is_end = jnp.logical_or(row == 0, row == 3)
@@ -154,11 +156,43 @@
     blocks = pl.ds(0, NZA)
     copy_a = pltpu.make_async_copy(a_ref.at[0, 0], own_a.at[blocks], local_sem.at[0])
     copy_b = pltpu.make_async_copy(b_ref.at[0, 0, 0], own_b.at[col], local_sem.at[1])
+
+    barrier = pltpu.get_barrier_semaphore()
+    for target in others():
+        pl.semaphore_signal(
+            barrier, inc=1, device_id={"col": target}, device_id_type=pl.DeviceIdType.MESH
+        )
+
+    @pl.when(is_end)
+    def _():
+        pl.semaphore_signal(
+            barrier, inc=1, device_id={"row": beside}, device_id_type=pl.DeviceIdType.MESH
+        )
+
+    @pl.when(is_middle)
+    def _():
+        for target in (outer, inner):
+            pl.semaphore_signal(
+                barrier, inc=1, device_id={"row": target}, device_id_type=pl.DeviceIdType.MESH
+            )
+
+    given = [
+        pltpu.make_async_copy(src, dst, in_sem.at[n])
+        for n, (src, dst) in enumerate(
+            (
+                (a_index_in, a_index), (a_live_in, a_live),
+                (b_index_in, b_index), (c_keep_in, c_keep),
+            )
+        )
+    ]
+    for copy in given:
+        copy.start()
     copy_a.start()
     copy_b.start()
-
-    lane = lax.broadcasted_iota(jnp.int32, (8, BS), 1)
-    table = jnp.full((8, BS), ZERO, jnp.int32)
+    for copy in given:
+        copy.wait()
+    lane = lax.broadcasted_iota(jnp.int32, (1, BS), 1)
+    table = jnp.full((1, BS), ZERO, jnp.int32)
     live = a_live[0, 0]
     for slot in range(NZA):
         place = a_index[0, 0, 0, slot] * KP + a_index[0, 0, 1, slot]
@@ -171,30 +205,18 @@
     own_bt[col] = table
     blank = jnp.zeros((BS, BS), jnp.bfloat16)
     own_a[ZERO] = blank
-    inner_a[ZERO] = blank
     outer_a[ZERO] = blank
     for n in range(NCH):
+        inner_a[n][ZERO] = blank[: CHUNKS[n]]
         far_a[n][ZERO] = blank[: CHUNKS[n]]
 
-    barrier = pltpu.get_barrier_semaphore()
-    for target in others():
-        pl.semaphore_signal(
-            barrier, inc=1, device_id={"col": target}, device_id_type=pl.DeviceIdType.MESH
-        )
 
     @pl.when(is_end)
     def _():
-        pl.semaphore_signal(
-            barrier, inc=1, device_id={"row": beside}, device_id_type=pl.DeviceIdType.MESH
-        )
         pl.semaphore_wait(barrier, 4)
 
     @pl.when(is_middle)
     def _():
-        for target in (outer, inner):
-            pl.semaphore_signal(
-                barrier, inc=1, device_id={"row": target}, device_id_type=pl.DeviceIdType.MESH
-            )
         pl.semaphore_wait(barrier, 5)
 
     def to_smem(src, dst, n):
@@ -210,20 +232,24 @@
                     block * hot
                 ).astype(jnp.bfloat16)
 
-    def picked(a_buf, tab, meta, panel, r):
+    def looked_up(tab, meta, panel):
+        places = [meta[panel, 0, B_INNER + slot] for slot in range(NZB)]
+        return [[tab[0, r * KP + place] for place in places] for r in range(MR)]
+
+    def picked(a_buf, slots):
         return jnp.concatenate(
-            [a_buf[tab[0, r * KP + meta[panel, 0, B_INNER + slot]]] for slot in range(NZB)],
-            axis=1,
-        )
-
-    def times(x, w_ref, at):
-        return jnp.dot(
-            x, w_ref[pl.ds(at * DEPTH, DEPTH), :], preferred_element_type=jnp.float32
-        )
+            [jnp.concatenate([a_buf[slot] for slot in line], axis=1) for line in slots], axis=0
+        )
+
+    def times(x, w_ref, at, count=1):
+        product = jnp.dot(
+            x, w_ref[pl.ds(at * DEPTH, count * DEPTH), :], preferred_element_type=jnp.float32
+        )
+        return product.reshape(MR, x.shape[0] // MR, WIDE)
 
     def store(r, start, size, value):
         for c in range(NC):
-            kept = value[:, c * BS : (c + 1) * BS] * c_keep[r, c].astype(jnp.float32)
+            kept = value[:, c * BS : (c + 1) * BS] * c_keep[c, r].astype(jnp.float32)
             o_ref[pl.ds(r * BS + start, size), pl.ds(c * BS, BS)] = kept.astype(jnp.bfloat16)
 
     @pl.when(is_end)
@@ -241,7 +267,7 @@
                     a_send.at[n], a_recv.at[n], beside,
                 )
             )
-        for send in sends:
+        for send in sends[: 2 + END_AHEAD]:
             send.start()
 
         def shared():
@@ -260,6 +286,9 @@
             for send in shared():
                 send.start()
 
+        for n in range(2 + END_AHEAD, len(sends)):
+            sends[n - END_AHEAD].wait_send()
+            sends[n].start()
         @pl.when(col != row)
         def _():
             to_col(own_bt.at[row], own_bt.at[row], bt_send.at[0, 0], bt_recv.at[0, row], col).wait_recv()
@@ -274,11 +303,7 @@
             load.wait()
         place_b(own_w, 0, own_b, own_bs, row)
 
-        def own_part(r, carry):
-            own_sum[r] = times(picked(own_a, own_st, own_bs, row, r), own_w, 0)
-            return carry
-
-        lax.fori_loop(0, MR, own_part, 0)
+        own_sum[...] = times(picked(own_a, looked_up(own_st, own_bs, row)), own_w, 0)
         for n in range(NCH):
             piece = pl.ds(STARTS[n], CHUNKS[n])
             to_row(
@@ -287,7 +312,7 @@
             ).wait_recv()
             for r in range(MR):
                 store(r, STARTS[n], CHUNKS[n], own_sum[r, piece, :] + sum_in[r, piece, :])
-        for send in sends:
+        for send in sends[:2] + sends[-END_AHEAD:]:
             send.wait_send()
 
         @pl.when(col == row)
@@ -297,10 +322,35 @@
 
     @pl.when(is_middle)
     def _():
-        sends = [
-            to_row(own_tab, inner_tab, tab_send.at[0], tab_recv.at[1], inner),
-            to_row(a_ref.at[0, 0], inner_a.at[blocks], a_send.at[NCH], a_recv.at[NCH], inner),
+        pieces = [pl.ds(start, size) for start, size in zip(STARTS, CHUNKS)]
+        mine = [
+            to_row(
+                a_ref.at[0, 0, :, pieces[n], :], inner_a[n].at[blocks],
+                a_send.at[n], a_recv.at[NCH + n], inner,
+            )
+            for n in range(NCH)
         ]
+        passed = [
+            to_row(
+                outer_a.at[blocks, pieces[n], :], far_a[n].at[blocks],
+                a_send.at[NCH + n], a_recv.at[2 * NCH + n], inner,
+            )
+            for n in range(NCH)
+        ]
+        queue = [(send, None) for send in mine[:AHEAD]]
+        for n in range(NCH):
+            queue.append((passed[n], n))
+            queue += [(send, None) for send in mine[AHEAD + n : AHEAD + n + 1]]
+
+        def advance(at):
+            queue[at - AHEAD][0].wait_send()
+            send, n = queue[at]
+            if n is not None:
+                part = outer_a.at[blocks, pieces[n], :]
+                to_row(part, part, a_send.at[NCH + n], a_recv.at[n], outer).wait_recv()
+            send.start()
+
+        sends = [to_row(own_tab, inner_tab, tab_send.at[0], tab_recv.at[1], inner)]
         for n, target in enumerate(others()):
             sends.append(
                 to_col(own_tab, own_bt.at[col], bt_send.at[0, n], bt_recv.at[0, col], target)
@@ -308,12 +358,8 @@
             sends.append(
                 to_col(b_ref.at[0, 0, 0], own_b.at[col], b_send.at[0, n], b_recv.at[0, col], target)
             )
-        for send in sends:
+        for send in sends[:1] + mine[:AHEAD] + sends[1:]:
             send.start()
-
-        to_row(outer_tab, outer_tab, tab_send.at[1], tab_recv.at[0], outer).wait_recv()
-        onward = [to_row(outer_tab, far_tab, tab_send.at[1], tab_recv.at[2], inner)]
-        onward[0].start()
 
         def passed_b():
             out = []
@@ -326,6 +372,9 @@
                 )
             return out
 
+        to_row(outer_tab, outer_tab, tab_send.at[1], tab_recv.at[0], outer).wait_recv()
+        onward = [to_row(outer_tab, far_tab, tab_send.at[1], tab_recv.at[2], inner)]
+        onward[0].start()
         to_row(outer_bt.at[col], outer_bt.at[col], tab_send.at[1], bt_recv.at[1, col], outer).wait_recv()
         to_row(outer_b.at[col], outer_b.at[col], tab_send.at[1], b_recv.at[1, col], outer).wait_recv()
 
@@ -334,13 +383,8 @@
             for send in passed_b():
                 send.start()
 
-        for n in range(NCH):
-            piece = pl.ds(STARTS[n], CHUNKS[n])
-            part = outer_a.at[blocks, piece, :]
-            to_row(part, part, a_send.at[n], a_recv.at[n], outer).wait_recv()
-            send = to_row(part, far_a[n].at[blocks], a_send.at[n], a_recv.at[NCH + 1 + n], inner)
-            send.start()
-            onward.append(send)
+        for at in range(AHEAD, EARLY):
+            advance(at)
 
         for source in others():
             to_col(own_bt.at[source], own_bt.at[source], bt_send.at[0, 0], bt_recv.at[0, source], col).wait_recv()
@@ -368,52 +412,51 @@
         copy_b.wait()
         for load in loads:
             load.wait()
-        for at, panel in enumerate(panels):
-            place_b(own_w, at, own_b, own_bs, panel)
-            if at < 3:
-                place_b(outer_w, at, outer_b, outer_bs, panel)
-
-        def own_part(r, carry):
-            own_sum[r] = times(
-                picked(own_a, own_st, own_bs, panels[0], r), own_w, 0
-            ) + times(picked(outer_a, outer_st, own_bs, panels[3], r), own_w, 3)
-            outer_sum[r] = times(picked(own_a, own_st, outer_bs, panels[0], r), outer_w, 0)
-            return carry
-
-        lax.fori_loop(0, MR, own_part, 0)
-        to_row(
-            inner_a.at[blocks], inner_a.at[blocks], a_send.at[0], a_recv.at[NCH], inner
-        ).wait_recv()
-
-        def inner_part(r, carry):
-            own_sum[r] += times(picked(inner_a, inner_st, own_bs, panels[1], r), own_w, 1)
-            outer_sum[r] += times(picked(inner_a, inner_st, outer_bs, panels[1], r), outer_w, 1)
-            return carry
-
-        lax.fori_loop(0, MR, inner_part, 0)
-
-        def far_part(n, w_ref, meta):
-            x = jnp.concatenate(
-                [picked(far_a[n], far_st, meta, panels[2], r) for r in range(MR)], axis=0
-            )
-            return times(x, w_ref, 2).reshape(MR, CHUNKS[n], WIDE)
-
+        tabs = (own_st, inner_st, far_st, outer_st)
+        own_slots = [looked_up(tab, own_bs, panel) for tab, panel in zip(tabs, panels)]
+        outer_slots = [looked_up(tab, outer_bs, panel) for tab, panel in zip(tabs[:3], panels)]
+        for at in range(3):
+            place_b(outer_w, at, outer_b, outer_bs, panels[at])
+        outer_sum[...] = times(picked(own_a, outer_slots[0]), outer_w, 0)
+
+        def from_inner(n, slots, w_ref):
+            x = jnp.concatenate([picked(inner_a[n], slots[1]), picked(far_a[n], slots[2])], axis=1)
+            return times(x, w_ref, 1, 2)
+
+        def finish(n):
+            total = own_sum[:, pieces[n], :] + from_inner(n, own_slots, own_w)
+            for r in range(MR):
+                store(r, STARTS[n], CHUNKS[n], total[r])
+
+        at = EARLY
         for n in range(NCH):
-            piece = pl.ds(STARTS[n], CHUNKS[n])
+            if at < len(queue):
+                advance(at)
+                at += 1
             to_row(
-                far_a[n].at[blocks], far_a[n].at[blocks], a_send.at[0], a_recv.at[NCH + 1 + n], inner
+                inner_a[n].at[blocks], inner_a[n].at[blocks], a_send.at[0], a_recv.at[NCH + n], inner
             ).wait_recv()
-            outer_sum[:, piece, :] += far_part(n, outer_w, outer_bs)
+            to_row(
+                far_a[n].at[blocks], far_a[n].at[blocks], a_send.at[0], a_recv.at[2 * NCH + n], inner
+            ).wait_recv()
+            outer_sum[:, pieces[n], :] += from_inner(n, outer_slots, outer_w)
             send = to_row(
-                outer_sum.at[:, piece, :], sum_in.at[:, piece, :],
+                outer_sum.at[:, pieces[n], :], sum_in.at[:, pieces[n], :],
                 sum_send.at[n], sum_recv.at[n], outer,
             )
             send.start()
             onward.append(send)
-            mine = own_sum[:, piece, :] + far_part(n, own_w, own_bs)
-            for r in range(MR):
-                store(r, STARTS[n], CHUNKS[n], mine[r])
-        for send in sends + onward:
+            if n == 0:
+                for at_w, panel in enumerate(panels):
+                    place_b(own_w, at_w, own_b, own_bs, panel)
+                own_sum[...] = times(picked(own_a, own_slots[0]), own_w, 0)
+            if n == NCH - 2:
+                own_sum[...] += times(picked(outer_a, own_slots[3]), own_w, 3)
+                for done in range(NCH - 2):
+                    finish(done)
+        finish(NCH - 2)
+        finish(NCH - 1)
+        for send in sends + onward + [entry[0] for entry in queue[-AHEAD:]]:
             send.wait_send()
 
         @pl.when(col != outer)
@@ -423,19 +466,18 @@
 
 
 def line_local(a_blocks, a_index, a_live, b_blocks, b_index, c_keep):
-    scalar = pl.BlockSpec(memory_space=pltpu.SMEM)
-    anywhere = pl.BlockSpec(memory_space=pl.ANY)
+    anywhere = pl.BlockSpec(memory_space=pltpu.HBM)
     dma = pltpu.SemaphoreType.DMA
     panel = pltpu.VMEM((NZA + 1, BS, BS), jnp.bfloat16)
-    meta = (8, BS)
+    meta = (1, BS)
     total = pltpu.VMEM((MR, BS, WIDE), jnp.float32)
     return pl.pallas_call(
         line_kernel,
         out_shape=jax.ShapeDtypeStruct((MR * BS, WIDE), jnp.bfloat16),
-        in_specs=[scalar] * 4 + [anywhere] * 2,
+        in_specs=[anywhere] * 6,
         out_specs=pl.BlockSpec(memory_space=pltpu.VMEM),
-        scratch_shapes=[panel] * 3
-        + [pltpu.VMEM((NZA + 1, size, BS), jnp.bfloat16) for size in CHUNKS]
+        scratch_shapes=[panel] * 2
+        + [[pltpu.VMEM((NZA + 1, size, BS), jnp.bfloat16) for size in CHUNKS]] * 2
         + [pltpu.VMEM((4, NZB, BS, BS), jnp.bfloat16)] * 2
         + [pltpu.VMEM((4 * DEPTH, WIDE), jnp.bfloat16), pltpu.VMEM((3 * DEPTH, WIDE), jnp.bfloat16)]
         + [total] * 3
@@ -445,14 +487,16 @@
         + [pltpu.SMEM((4,) + meta, jnp.int32)] * 2
         + [
             dma((2,)), dma((6,)),
-            dma((NCH + 1,)), dma((2 * NCH + 1,)), dma((2,)), dma((3,)),
+            dma((2 * NCH,)), dma((3 * NCH,)), dma((2,)), dma((3,)),
             dma((2, 3)), dma((2, 4)), dma((2, 3)), dma((2, 4)),
             dma((NCH,)), dma((NCH,)),
-        ],
+        ]
+        + [pltpu.SMEM(one.shape, jnp.int32) for one in (a_index, a_live, b_index, c_keep.T)]
+        + [dma((4,))],
         compiler_params=pltpu.CompilerParams(
-            collective_id=0, has_side_effects=True, vmem_limit_bytes=32 * 1024 * 1024
+            collective_id=0, has_side_effects=True, vmem_limit_bytes=54630 * 1024
         ),
-    )(a_index, a_live, b_index, c_keep, a_blocks, b_blocks)
+    )(a_index, a_live, b_index, c_keep.T, a_blocks, b_blocks)
 
 
 def solution(mesh):

time: 40.5 us -> 36.4 us (0.90)
  Pallas kernels: 36.3 us -> 33.3 us
  local copies, waits for them, and re-layouts: 3.33 us -> 2.26 us
    pallas_call x1, Pallas kernels: 36.3 us -> 33.3 us  [line_local(): pl.pallas_call(line_kernel, out_shape=jax.ShapeDtypeStruct((MR * BS, WIDE...]
    unnamed x12 -> x9, local copies, waits for them, and re-layouts: 3.33 us -> 2.26 us
where the time goes in v2:
time: 36.4 us; the launch traced here: 36.2 us
  Pallas kernels  33.3 us (91%)
  local copies, waits for them, and re-layouts  2.26 us (6%)
  between operations  0.71 us (2%)
    pallas_call x1, Pallas kernels, line_local(): pl.pallas_call(line_kernel, out_shape=jax.ShapeDtypeStruct((MR * BS, WIDE...  33.3 us
    unnamed x9, local copies, waits for them, and re-layouts  2.26 us

profile of v2, /device:TPU:0, one launch (start us, length us, event | category | flops | bytes accessed | tf_op | source)
XLA Modules:
  0.0 36.2 jit_solution(5158089445522246770)
XLA Ops:
  0.0 0.0 copy-start.2
  0.0 0.0 copy-start.3
  0.7 0.0 copy-start.1
  0.7 0.0 copy-done.2
  0.7 0.0 copy-done.3
  0.7 0.7 %copy-done.1 = s32[1,1,2,16]{3,2,1,0:T(2,128)S(1)} copy-done((s32[1,1,2,16]{3,2,1,0:T(2,128)S(1)}, s32[1,1,2,16]{3,2,1,0:T(2,128)}, u32[]{:S(2)}) %copy-start.1) | copy-done | bytes 152
  1.4 0.0 copy-start
  1.4 0.9 %copy-done = bf16[1,1,1,3,128,128]{5,4,3,2,1,0:T(8,128)(2,1)S(1)} copy-done((bf16[1,1,1,3,128,128]{5,4,3,2,1,0:T(8,128)(2,1)S(1)}, bf16[1,1,1,3,128,128]{5,4,3,2,1,0:T(8,128)(2,1)}, u32[]{:S(2)}) %copy-start) | copy-done | bytes 98328
  2.3 33.3 %shard_map.64 = bf16[512,256]{1,0:T(8,128)(2,1)S(1)} custom-call(s32[1,1,2,16]{3,2,1,0:T(2,128)S(1)} %copy-done.1, s32[1,1]{1,0:T(1,128)S(6)} %copy.8.a_live_in, s32[1,1,1,2,3]{4,3,2,1,0:T(2,128)S(1)} %copy-done.2, s32[2,4]{1,0:T(2,128)S(1)} %bitcast.1, bf16[1,1,16,128,128]{4,3,2,1,0:T(8,128)(2,1)} %a_ref.1, bf16[1,1,1,3,128,128]{5,4,3,2,1,0:T(8,128)(2,1)S(1)} %copy-done), custom_call_target="tpu_custom_call" | custom-call | tf_op jit(solution)/shard_map/pallas_call | solution.py:474
  35.5 0.7 %copy.9 = bf16[512,256]{1,0:T(8,128)(2,1)} copy(bf16[512,256]{1,0:T(8,128)(2,1)S(1)} %shard_map.64) | data formatting | bytes 524288
Async XLA Ops:
  0.0 0.7 %copy-start.2 = (s32[1,1,1,2,3]{4,3,2,1,0:T(2,128)S(1)}, s32[1,1,1,2,3]{4,3,2,1,0:T(2,128)}, u32[]{:S(2)}) copy-start(s32[1,1,1,2,3]{4,3,2,1,0:T(2,128)} %b_index_in.1) | copy-start | bytes 76
  0.0 0.7 %copy-start.3 = (s32[4,2]{0,1:T(2,128)S(1)}, s32[4,2]{0,1:T(2,128)}, u32[]{:S(2)}) copy-start(s32[4,2]{0,1:T(2,128)} %param.11) | copy-start | bytes 100
  0.7 0.7 %copy-start.1 = (s32[1,1,2,16]{3,2,1,0:T(2,128)S(1)}, s32[1,1,2,16]{3,2,1,0:T(2,128)}, u32[]{:S(2)}) copy-start(s32[1,1,2,16]{3,2,1,0:T(2,128)} %a_index_in.1) | copy-start | bytes 388
  1.4 0.9 %copy-start = (bf16[1,1,1,3,128,128]{5,4,3,2,1,0:T(8,128)(2,1)S(1)}, bf16[1,1,1,3,128,128]{5,4,3,2,1,0:T(8,128)(2,1)}, u32[]{:S(2)}) copy-start(bf16[1,1,1,3,128,128]{5,4,3,2,1,0:T(8,128)(2,1)} %b_ref.1) | copy-start | bytes 294916

commit v3 on v2

--- a/solution.py
+++ b/solution.py
@@ -473,7 +473,7 @@
     total = pltpu.VMEM((MR, BS, WIDE), jnp.float32)
     return pl.pallas_call(
         line_kernel,
-        out_shape=jax.ShapeDtypeStruct((MR * BS, WIDE), jnp.bfloat16),
+        out_shape=pltpu.VMEM((MR * BS, WIDE), jnp.bfloat16),
         in_specs=[anywhere] * 6,
         out_specs=pl.BlockSpec(memory_space=pltpu.VMEM),
         scratch_shapes=[panel] * 2
@@ -494,7 +494,7 @@
         + [pltpu.SMEM(one.shape, jnp.int32) for one in (a_index, a_live, b_index, c_keep.T)]
         + [dma((4,))],
         compiler_params=pltpu.CompilerParams(
-            collective_id=0, has_side_effects=True, vmem_limit_bytes=54630 * 1024
+            collective_id=0, has_side_effects=True, vmem_limit_bytes=60 * 1024 * 1024
         ),
     )(a_index, a_live, b_index, c_keep.T, a_blocks, b_blocks)
 

time: 36.4 us -> 34.8 us (0.956)
  local copies, waits for them, and re-layouts: 2.26 us -> 0.71 us
    unnamed x9 -> x1, local copies, waits for them, and re-layouts: 2.26 us -> 0.71 us
where the time goes in v3:
time: 34.8 us; the launch traced here: 34.6 us
  Pallas kernels  33.2 us (95%)
  local copies, waits for them, and re-layouts  0.71 us (2%)
  between operations  0.66 us (2%)
    pallas_call x1, Pallas kernels, line_local(): pl.pallas_call(line_kernel, out_shape=pltpu.VMEM((MR * BS, WIDE), jnp.bfl...  33.2 us
    unnamed x1, local copies, waits for them, and re-layouts  0.71 us

profile of v3, /device:TPU:0, one launch (start us, length us, event | category | flops | bytes accessed | tf_op | source)
XLA Modules:
  0.0 34.6 jit_solution(14860335477989868623)
XLA Ops:
  0.7 33.2 %shard_map.64 = bf16[512,256]{1,0:T(8,128)(2,1)S(1)} custom-call(s32[1,1,2,16]{3,2,1,0:T(2,128)} %a_index_in.1, s32[1,1]{1,0:T(1,128)S(6)} %copy.9.a_live_in, s32[1,1,1,2,3]{4,3,2,1,0:T(2,128)} %b_index_in.1, s32[2,4]{1,0:T(2,128)} %bitcast.1, bf16[1,1,16,128,128]{4,3,2,1,0:T(8,128)(2,1)} %a_ref.1, bf16[1,1,1,3,128,128]{5,4,3,2,1,0:T(8,128)(2,1)} %b_ref.1), custom_call_target="tpu_custom_call" | custom-call | tf_op jit(solution)/shard_map/pallas_call | solution.py:474
  33.9 0.7 %copy.8 = bf16[512,256]{1,0:T(8,128)(2,1)} copy(bf16[512,256]{1,0:T(8,128)(2,1)S(1)} %shard_map.64) | data formatting | bytes 524288

commit v4 on v3

--- a/solution.py
+++ b/solution.py
@@ -112,7 +112,7 @@
 NCH = len(CHUNKS)
 EARLY = 8
 AHEAD = 3
-END_AHEAD = 2
+END_AHEAD = 1
 ZERO = NZA
 B_INNER = 64
 B_COLUMN = 72

time: 34.8 us -> 34.7 us (level)
  no operation moved by 1% of the time
where the time goes in v4:
time: 34.7 us; the launch traced here: 34.5 us
  Pallas kernels  33.2 us (96%)
  local copies, waits for them, and re-layouts  0.71 us (2%)
  between operations  0.66 us (2%)
    pallas_call x1, Pallas kernels, line_local(): pl.pallas_call(line_kernel, out_shape=pltpu.VMEM((MR * BS, WIDE), jnp.bfl...  33.2 us
    unnamed x1, local copies, waits for them, and re-layouts  0.71 us

profile of v4, /device:TPU:0, one launch (start us, length us, event | category | flops | bytes accessed | tf_op | source)
XLA Modules:
  0.0 34.5 jit_solution(14822206047024273485)
XLA Ops:
  0.7 33.2 %shard_map.64 = bf16[512,256]{1,0:T(8,128)(2,1)S(1)} custom-call(s32[1,1,2,16]{3,2,1,0:T(2,128)} %a_index_in.1, s32[1,1]{1,0:T(1,128)S(6)} %copy.9.a_live_in, s32[1,1,1,2,3]{4,3,2,1,0:T(2,128)} %b_index_in.1, s32[2,4]{1,0:T(2,128)} %bitcast.1, bf16[1,1,16,128,128]{4,3,2,1,0:T(8,128)(2,1)} %a_ref.1, bf16[1,1,1,3,128,128]{5,4,3,2,1,0:T(8,128)(2,1)} %b_ref.1), custom_call_target="tpu_custom_call" | custom-call | tf_op jit(solution)/shard_map/pallas_call | solution.py:474
  33.8 0.7 %copy.8 = bf16[512,256]{1,0:T(8,128)(2,1)} copy(bf16[512,256]{1,0:T(8,128)(2,1)S(1)} %shard_map.64) | data formatting | bytes 524288
